TPU v7x, 32 devices: a whole 2x2x4 slice. The times are simulated.
32 devices in a mesh: grp: 2 (over y), tok: 4 (over x, core), mdl: 4 (over z).
Axes of the slice: x: 2, y: 2, z: 4, core: 2. Of those that a mesh axis runs over, the one named last changes fastest.
Arguments:
- tokens: bfloat16 [1024, 8192], P(('grp', 'tok'), 'mdl'), parts along dimension 0, may hold values from -6 to 6
- in_weight: bfloat16 [4096, 3, 8192], P('tok', None, 'mdl'), may hold values from -0.0625 to 0.0625
- short_weight: float32 [4096, 3, 3], P(('tok', 'mdl')), may hold values from -3 to 3
- long_filter: float32 [256, 128], P(('tok', 'mdl')), may hold values from -0.6 to 0.6
- skip_bias: float32 [4096], P(('tok', 'mdl')), may hold values from 0.5 to 1.5
Outputs:
- mixed: bfloat16 [4096, 1024], P('tok', ('grp', 'mdl')), parts along dimension 1
There are 2 independent parts, one for each index of `grp`. A program takes and returns all parts, laid end to end along the dimension named above; an argument that names none is the same for every part. Nothing has to cross between parts.
All inputs are finite; a program needn't handle non-finite values.
Results may differ from a plain program's by a relative error of at most 0.017.
Values may be sent and summed in bfloat16 or wider, within the bound.
A program may use at most 128 MiB of HBM per device.

v0:
```python
import jax
import jax.numpy as jnp
from jax import lax
from jax.sharding import PartitionSpec as P


def toeplitz_rows(padded_taps):
    group_count, padded_len = padded_taps.shape
    tap_count = (padded_len - 1) // 2
    tiled = jnp.tile(padded_taps, (1, tap_count))
    trimmed = tiled[:, : tap_count * (padded_len - 1)]
    shaped = trimmed.reshape(group_count, tap_count, padded_len - 1)
    return shaped[:, :, tap_count : 2 * tap_count]


def long_convolution(product, long_filter):
    channel_count, seq_length = product.shape
    group_count, tap_count = long_filter.shape
    near_pad = jnp.concatenate(
        [
            jnp.zeros((group_count, tap_count), jnp.float32),
            long_filter,
            jnp.zeros((group_count, 1), jnp.float32),
        ],
        1,
    )
    far_pad = jnp.concatenate(
        [long_filter, jnp.zeros((group_count, tap_count + 1), jnp.float32)], 1
    )
    near_taps = toeplitz_rows(near_pad)
    far_taps = toeplitz_rows(far_pad)
    blocks = product.reshape(
        group_count, channel_count // group_count, seq_length // tap_count, tap_count
    )
    earlier = jnp.pad(blocks, ((0, 0), (0, 0), (1, 0), (0, 0)))[:, :, :-1]
    filtered = jnp.einsum("gcna,gab->gcnb", blocks, near_taps, precision=lax.Precision.HIGHEST)
    filtered = filtered + jnp.einsum(
        "gcna,gab->gcnb", earlier, far_taps, precision=lax.Precision.HIGHEST
    )
    return filtered.reshape(channel_count, seq_length)


def local(tokens, in_weight, short_weight, long_filter, skip_bias):
    mdl_count = lax.axis_size("mdl")
    local_chans, stream_count, feature_part = in_weight.shape
    weight_rows = in_weight.reshape(local_chans * stream_count, feature_part)
    gathered = lax.all_gather(tokens, "tok", axis=0, tiled=True)
    seq_length = gathered.shape[0]
    slot_rows = local_chans * stream_count // mdl_count
    token_block = lax.psum_scatter(
        lax.dot_general(
            gathered, weight_rows, (((1,), (1,)), ((), ())), preferred_element_type=jnp.float32
        ).astype(jnp.bfloat16),
        "mdl",
        scatter_dimension=0,
        tiled=True,
    ).astype(jnp.float32)
    regrouped = lax.all_to_all(
        token_block.astype(jnp.bfloat16), "mdl", split_axis=1, concat_axis=0, tiled=True
    ).astype(token_block.dtype)
    projected = regrouped.T
    channel_count = slot_rows // stream_count
    streams = projected.reshape(channel_count, stream_count, seq_length)
    padded = jnp.pad(streams, ((0, 0), (0, 0), (2, 0)))
    featured = jnp.zeros_like(streams)
    for shift_index in range(3):
        featured = (
            featured
            + short_weight[:, :, shift_index : shift_index + 1]
            * padded[:, :, 2 - shift_index : 2 - shift_index + seq_length]
        )
    queries = featured[:, 0]
    product = featured[:, 1] * featured[:, 2]
    filtered = long_convolution(product, long_filter)
    mixed_out = (queries * (filtered + skip_bias[:, None] * product)).astype(jnp.bfloat16)
    return lax.all_to_all(mixed_out, "mdl", split_axis=1, concat_axis=0, tiled=True)


def solution(mesh):
    in_specs = (
        P(("grp", "tok"), "mdl"),
        P("tok", None, "mdl"),
        P(("tok", "mdl"), None, None),
        P(("tok", "mdl"), None),
        P(("tok", "mdl")),
    )
    out_specs = P("tok", ("grp", "mdl"))
    return jax.shard_map(local, mesh=mesh, in_specs=in_specs, out_specs=out_specs, check_vma=False)
```

profile of v0, /device:TPU:0, one launch (start us, length us, event | category | flops | bytes accessed | tf_op | source)
XLA Modules:
  0.0 194.2 jit_solution(13229022793350379808)
XLA Ops:
  6.5 0.7 all-gather.2.cloned.1.call-update
  7.3 18.8 %copy.22 = bf16[1024,3,2048]{2,1,0:T(4,128)(2,1)} copy(bf16[1024,3,2048]{2,0,1:T(8,128)(2,1)} %param.6) | data formatting | bytes 25165824 | tf_op args[1]
  26.1 31.3 %reshape.49 = bf16[3072,2048]{1,0:T(8,128)(2,1)} reshape(bf16[1024,3,2048]{2,1,0:T(4,128)(2,1)} %copy.22) | data formatting | bytes 25165824 | tf_op jit(solution)/shard_map/reshape | solution.py:46
  57.5 13.0 %convolution_convert_fusion = bf16[512,3072]{1,0:T(8,128)(2,1)} fusion(bf16[512,2048]{1,0:T(8,128)(2,1)} %all-gather.2.cloned.1.call-done, bf16[3072,2048]{1,0:T(8,128)(2,1)} %reshape.49), kind=kOutput, calls=%fused_computation | convolution fusion | flops 6444023808 | bytes 17825792 | tf_op jit(solution)/shard_map/dot_general | solution.py:51
  70.5 63.1 %reduce-scatter.2.cloned.1.call-done = bf16[128,3072]{1,0:T(8,128)(2,1)} async-done(((bf16[512,3072]{1,0:T(8,128)(2,1)}), bf16[128,3072]{1,0:T(8,128)(2,1)}) %reduce-scatter.2.cloned.1.call-update) | async-done | bytes 786448 | tf_op jit(solution)/shard_map/reduce_scatter | solution.py:50
  133.6 2.1 %copy.47 = bf16[16,4,8,768]{3,2,0,1:T(8,128)(2,1)} copy(bf16[16,4,8,768]{3,2,1,0:T(8,128)(2,1)} %bitcast.46) | data formatting | bytes 1572864 | tf_op jit(solution)/shard_map/all_to_all | solution.py:58
  135.6 4.4 %all-to-all-start = ((bf16[128,4,768]{2,0,1:T(8,128)(2,1)}), bf16[128,4,768]{2,0,1:T(8,128)(2,1)}, u32[]{:S(2)}, u32[]{:S(2)}) async-start(bf16[128,4,768]{2,0,1:T(8,128)(2,1)} %bitcast.34), calls=%async_computation.1 | async-start | bytes 1572864 | tf_op jit(solution)/shard_map/all_to_all | solution.py:58
  141.4 2.5 %tile.9 = f32[16,32896]{1,0:T(8,128)} reshape(f32[16,128,257]{2,1,0:T(8,128)S(1)} %tile.8) | data formatting | bytes 4210688 | tf_op jit(solution)/shard_map/tile | solution.py:10
  143.9 1.6 slice-done
  145.4 1.9 copy.40
  147.6 2.5 %tile.21 = f32[16,32896]{1,0:T(8,128)} reshape(f32[16,128,257]{2,1,0:T(8,128)S(1)} %tile.20) | data formatting | bytes 4210688 | tf_op jit(solution)/shard_map/tile | solution.py:10
  150.1 1.6 slice-done.1
  151.7 2.0 %copy.41 = f32[2,8,128,256]{3,2,1,0:T(8,128)} copy(f32[2,8,128,256]{3,1,2,0:T(8,128)S(1)} %bitcast.36) | data formatting | bytes 4194304
  153.6 6.7 %all-to-all-done = bf16[128,4,768]{2,0,1:T(8,128)(2,1)} async-done(((bf16[128,4,768]{2,0,1:T(8,128)(2,1)}), bf16[128,4,768]{2,0,1:T(8,128)(2,1)}, u32[]{:S(2)}, u32[]{:S(2)}) %all-to-all-start) | async-done | bytes 786464 | tf_op jit(solution)/shard_map/all_to_all | solution.py:58
  160.3 1.3 reshape.60
  161.6 1.7 copy.24
  163.3 2.5 %reshape.56 = f32[256,3,512]{2,1,0:T(4,128)S(1)} reshape(f32[768,512]{1,0:T(8,128)} %copy.24) | data formatting | bytes 3145728 | tf_op jit(solution)/shard_map/reshape | solution.py:63
  165.8 3.5 %fusion.2 = f32[256,3,512]{2,1,0:T(4,128)S(1)} fusion(f32[256,3,512]{2,1,0:T(4,128)S(1)} %reshape.56, f32[256,3]{1,0:T(8,128)S(1)} %bitcast.49, f32[256,3]{1,0:T(8,128)S(1)} %bitcast.48, f32[256,3]{1,0:T(8,128)S(1)} %bitcast.47), kind=kLoop, calls=%fused_computation.5 | loop fusion | flops 1966080 | bytes 3154944 | tf_op jit(solution)/shard_map/add | solution.py:68
  169.3 1.0 slice_multiply_fusion
  170.4 1.2 copy.31
  171.6 1.1 fusion.4
  173.2 1.2 convolution_add_fusion
  175.5 11.0 %all_to_all.29 = bf16[256,4,128]{0,2,1:T(8,128)(2,1)S(1)} all-to-all(bf16[256,4,128]{0,2,1:T(8,128)(2,1)S(1)} %multiply_convert_fusion), channel_id=1, replica_groups=mesh['grp'=2,'tok'=4,'mdl'=4] {'mdl'}, dimensions={1} | all-to-all | bytes 524288 | tf_op jit(solution)/shard_map/all_to_all | solution.py:76
  186.5 0.8 copy.33
  (34 shorter events, 3.2 us)
Async XLA Ops:
  6.5 50.9 %all-gather.2.cloned.1.call-start = ((), (), s32[]{:S(2)}) async-start(), calls=%async_computation.3 | async-start | bytes 2621440 | tf_op jit(solution)/shard_map/all_gather | solution.py:47
  7.3 126.3 %reduce-scatter.2.cloned.1.call-start = ((), (), s32[]{:S(2)}) async-start(), calls=%async_computation.4 | async-start | bytes 3932160 | tf_op jit(solution)/shard_map/reduce_scatter | solution.py:50
  70.4 69.6 %copy-start.5 = (f32[256,3,3]{0,2,1:T(4,128)S(1)}, f32[256,3,3]{0,2,1:T(4,128)}, u32[]{:S(2)}) copy-start(f32[256,3,3]{0,2,1:T(4,128)} %param.7) | copy-start | bytes 27652
  70.4 70.1 %copy-start.4 = (f32[16,128]{1,0:T(8,128)S(1)}, f32[16,128]{1,0:T(8,128)}, u32[]{:S(2)}) copy-start(f32[16,128]{1,0:T(8,128)} %param.8) | copy-start | bytes 24580
  135.6 24.7 %all-to-all-start = ((bf16[128,4,768]{2,0,1:T(8,128)(2,1)}), bf16[128,4,768]{2,0,1:T(8,128)(2,1)}, u32[]{:S(2)}, u32[]{:S(2)}) async-start(bf16[128,4,768]{2,0,1:T(8,128)(2,1)} %bitcast.34), calls=%async_computation.1 | async-start | bytes 1572864 | tf_op jit(solution)/shard_map/all_to_all | solution.py:58
  143.8 1.6 slice-start
  145.4 1.9 copy-start.3
  150.1 1.6 slice-start.1
  169.3 2.2 %copy-start = (f32[2,8,128,256]{3,2,1,0:T(8,128)S(1)}, f32[2,8,128,256]{3,2,1,0:T(8,128)}, u32[]{:S(2)}) copy-start(f32[2,8,128,256]{3,2,1,0:T(8,128)} %copy.40) | copy-start | bytes 6291460
  171.6 1.6 copy-start.1
  174.4 1.0 copy-start.2
  174.4 1.0 copy-start.6
Sparse Core Ops, SparseCore 0:
  8.9 25.2 all-gather.1
  70.6 62.9 reduce-scatter.1
where the time goes:
time: 195 us; the launch traced here: 194 us
  local copies, waits for them, and re-layouts  72.9 us (37%)
  waiting for transfers between devices  70.5 us (36%)
  matrix products  15.2 us (8%)
  between operations  13.6 us (7%)
  blocking collectives  11 us (6%)
  other arithmetic  6.51 us (3%)
  starting transfers between devices  4.42 us (2%)
    reduce_scatter x1, waiting for transfers between devices, local(): lax.psum_scatter(lax.dot_general(gathered, weight_rows, (((1,), (1,)), ((...  63.1 us
    reshape x1, local copies, waits for them, and re-layouts, local(): weight_rows = in_weight.reshape(local_chans * stream_count, feature_part)  31.3 us
    unnamed x17, local copies, waits for them, and re-layouts  23.6 us
    dot_general x1, matrix products, local(): lax.dot_general(gathered, weight_rows, (((1,), (1,)), ((), ())), preferre...  13 us
    all_to_all x1, blocking collectives, local(): lax.all_to_all(mixed_out, 'mdl', split_axis=1, concat_axis=0, tiled=True)  11 us
    all_to_all x1, waiting for transfers between devices, local(): lax.all_to_all(token_block.astype(jnp.bfloat16), 'mdl', split_axis=1, con...  6.71 us
    another operation x4, local copies, waits for them, and re-layouts, toeplitz_rows(): tiled = jnp.tile(padded_taps, (1, tap_count))  5.39 us
    all_to_all x1, starting transfers between devices, local(): lax.all_to_all(token_block.astype(jnp.bfloat16), 'mdl', split_axis=1, con...  4.38 us
  transfers between devices with their start and end apart: 3, of which 2 were waited for; matrix products, arithmetic and copies ran while one was open for 31% of the time, Pallas kernels for 0%

commit v1 on v0

--- a/solution.py
+++ b/solution.py
@@ -43,36 +43,28 @@
 def local(tokens, in_weight, short_weight, long_filter, skip_bias):
     mdl_count = lax.axis_size("mdl")
     local_chans, stream_count, feature_part = in_weight.shape
-    weight_rows = in_weight.reshape(local_chans * stream_count, feature_part)
+    channel_count = local_chans // mdl_count
     gathered = lax.all_gather(tokens, "tok", axis=0, tiled=True)
     seq_length = gathered.shape[0]
-    slot_rows = local_chans * stream_count // mdl_count
-    token_block = lax.psum_scatter(
-        lax.dot_general(
-            gathered, weight_rows, (((1,), (1,)), ((), ())), preferred_element_type=jnp.float32
-        ).astype(jnp.bfloat16),
-        "mdl",
-        scatter_dimension=0,
-        tiled=True,
-    ).astype(jnp.float32)
-    regrouped = lax.all_to_all(
-        token_block.astype(jnp.bfloat16), "mdl", split_axis=1, concat_axis=0, tiled=True
-    ).astype(token_block.dtype)
-    projected = regrouped.T
-    channel_count = slot_rows // stream_count
-    streams = projected.reshape(channel_count, stream_count, seq_length)
+    weight_rows = in_weight.transpose(1, 0, 2).reshape(stream_count * local_chans, feature_part)
+    partial = lax.dot_general(
+        weight_rows, gathered, (((1,), (1,)), ((), ())), preferred_element_type=jnp.float32
+    ).astype(jnp.bfloat16)
+    partial = partial.reshape(stream_count, mdl_count, channel_count, seq_length)
+    streams = lax.psum_scatter(partial, "mdl", scatter_dimension=1, tiled=True)
+    streams = streams.reshape(stream_count, channel_count, seq_length).astype(jnp.float32)
+    taps = short_weight.transpose(1, 2, 0)
     padded = jnp.pad(streams, ((0, 0), (0, 0), (2, 0)))
     featured = jnp.zeros_like(streams)
     for shift_index in range(3):
         featured = (
             featured
-            + short_weight[:, :, shift_index : shift_index + 1]
+            + taps[:, shift_index, :, None]
             * padded[:, :, 2 - shift_index : 2 - shift_index + seq_length]
         )
-    queries = featured[:, 0]
-    product = featured[:, 1] * featured[:, 2]
+    product = featured[1] * featured[2]
     filtered = long_convolution(product, long_filter)
-    mixed_out = (queries * (filtered + skip_bias[:, None] * product)).astype(jnp.bfloat16)
+    mixed_out = (featured[0] * (filtered + skip_bias[:, None] * product)).astype(jnp.bfloat16)
     return lax.all_to_all(mixed_out, "mdl", split_axis=1, concat_axis=0, tiled=True)
 
 

time: 195 us -> 136 us (0.70)
  local copies, waits for them, and re-layouts: 72.9 us -> 19.8 us
  starting transfers between devices: 4.42 us -> 0.04 us
  waiting for transfers between devices: 70.5 us -> 74.8 us
  other arithmetic: 6.51 us -> 2.76 us
  matrix products: 15.2 us -> 12.6 us
    reshape x3 -> x1, local copies, waits for them, and re-layouts: 35.5 us -> 2.79 us  [local(): partial.reshape(stream_count, mdl_count, channel_count, seq_length)]
    all_gather x1, waiting for transfers between devices: 0.01 us -> 26.9 us  [local(): gathered = lax.all_gather(tokens, 'tok', axis=0, tiled=True)]
    unnamed x17 -> x16, local copies, waits for them, and re-layouts: 23.6 us -> 5.14 us
    reduce_scatter x1, waiting for transfers between devices: 63.1 us -> 47.1 us  [local(): streams = lax.psum_scatter(partial, 'mdl', scatter_dimension=1, tiled=True)]
    all_to_all x1 -> x0, waiting for transfers between devices: 6.71 us -> none  [local(): lax.all_to_all(token_block.astype(jnp.bfloat16), 'mdl', split_axis=1, con...]
    all_to_all x1 -> x0, starting transfers between devices: 4.38 us -> none  [local(): lax.all_to_all(token_block.astype(jnp.bfloat16), 'mdl', split_axis=1, con...]
    add x1, other arithmetic: 3.5 us -> 0.46 us  [local(): featured + taps[:, shift_index, :, None] * padded[:, :, 2 - shift_index:2...]
    dot_general x1, matrix products: 13 us -> 10.4 us  [local(): lax.dot_general(weight_rows, gathered, (((1,), (1,)), ((), ())), preferre...]
  transfers between devices with their start and end apart: 3 -> 2, of which waited for: 2 -> 2; matrix products, arithmetic and copies ran while one was open for 31% -> 7% of each run, Pallas kernels for 0% -> 0%
where the time goes in v1:
time: 136 us
  waiting for transfers between devices  74.8 us (55%)
  local copies, waits for them, and re-layouts  19.8 us (15%)
  between operations  13.6 us (10%)
  matrix products  12.6 us (9%)
  blocking collectives  12.4 us (9%)
  other arithmetic  2.76 us (2%)
    reduce_scatter x1, waiting for transfers between devices, local(): streams = lax.psum_scatter(partial, 'mdl', scatter_dimension=1, tiled=True)  47.1 us
    all_gather x1, waiting for transfers between devices, local(): gathered = lax.all_gather(tokens, 'tok', axis=0, tiled=True)  26.9 us
    all_to_all x1, blocking collectives, local(): lax.all_to_all(mixed_out, 'mdl', split_axis=1, concat_axis=0, tiled=True)  12.4 us
    dot_general x1, matrix products, local(): lax.dot_general(weight_rows, gathered, (((1,), (1,)), ((), ())), preferre...  10.4 us
    another operation x4, local copies, waits for them, and re-layouts, toeplitz_rows(): tiled = jnp.tile(padded_taps, (1, tap_count))  5.41 us
    unnamed x16, local copies, waits for them, and re-layouts  5.14 us
    slice x4, local copies, waits for them, and re-layouts, toeplitz_rows(): trimmed = tiled[:, :tap_count * (padded_len - 1)]  3.18 us
    reshape x1, local copies, waits for them, and re-layouts, local(): partial.reshape(stream_count, mdl_count, channel_count, seq_length)  2.79 us
  transfers between devices with their start and end apart: 2, of which 2 were waited for; matrix products, arithmetic and copies ran while one was open for 7% of the time, Pallas kernels for 0%

profile of v1, /device:TPU:0, one launch (start us, length us, event | category | flops | bytes accessed | tf_op | source)
XLA Modules:
  0.0 136.0 jit_solution(15679690224201385943)
XLA Ops:
  6.5 0.7 all-gather.2.cloned.1.call-update
  7.3 26.9 %all-gather.2.cloned.1.call-done = bf16[512,2048]{1,0:T(8,128)(2,1)} async-done(((bf16[128,2048]{1,0:T(8,128)(2,1)}), bf16[512,2048]{1,0:T(8,128)(2,1)}) %all-gather.2.cloned.1.call-update) | async-done | bytes 2097168 | tf_op jit(solution)/shard_map/all_gather | solution.py:47
  34.2 10.4 %convolution_convert_fusion = bf16[3072,512]{1,0:T(8,128)(2,1)S(1)} fusion(bf16[3072,2048]{1,0:T(8,128)(2,1)} %bitcast.48, bf16[512,2048]{1,0:T(8,128)(2,1)} %all-gather.2.cloned.1.call-done), kind=kOutput, calls=%fused_computation | convolution fusion | flops 6444023808 | bytes 17825792 | tf_op jit(solution)/shard_map/dot_general | solution.py:50
  44.6 2.8 %copy.18 = bf16[3,4,256,512]{2,3,0,1:T(8,128)(2,1)} copy(bf16[3,4,256,512]{3,2,1,0:T(8,128)(2,1)S(1)} %bitcast.42) | data formatting | bytes 6291456 | tf_op jit(solution)/shard_map/reshape | solution.py:53
  47.4 0.7 copy-done.4
  48.2 0.2 tile.8
  48.4 2.5 %tile.9 = f32[16,32896]{1,0:T(8,128)} reshape(f32[16,128,257]{2,1,0:T(8,128)S(1)} %tile.8) | data formatting | bytes 4210688 | tf_op jit(solution)/shard_map/tile | solution.py:10
  50.9 1.6 %slice-done = f32[16,32768]{1,0:T(8,128)S(1)} async-done(((f32[16,32896]{1,0:T(8,128)}), f32[16,32768]{1,0:T(8,128)S(1)}, s32[]{:S(2)}) %slice-start) | async-done | bytes 2097176 | tf_op jit(solution)/shard_map/slice | solution.py:11
  52.5 2.0 %copy.30 = f32[2,8,128,256]{3,2,1,0:T(8,128)} copy(f32[2,8,128,256]{3,1,2,0:T(8,128)S(1)} %bitcast.37) | data formatting | bytes 4194304
  54.5 0.2 tile.20
  54.7 2.5 %tile.21 = f32[16,32896]{1,0:T(8,128)} reshape(f32[16,128,257]{2,1,0:T(8,128)S(1)} %tile.20) | data formatting | bytes 4210688 | tf_op jit(solution)/shard_map/tile | solution.py:10
  57.2 1.6 %slice-done.1 = f32[16,32768]{1,0:T(8,128)S(1)} async-done(((f32[16,32896]{1,0:T(8,128)}), f32[16,32768]{1,0:T(8,128)S(1)}, s32[]{:S(2)}) %slice-start.1) | async-done | bytes 2097176 | tf_op jit(solution)/shard_map/slice | solution.py:11
  58.8 2.0 %copy.31 = f32[2,8,128,256]{3,2,1,0:T(8,128)} copy(f32[2,8,128,256]{3,1,2,0:T(8,128)S(1)} %bitcast.38) | data formatting | bytes 4194304
  60.7 47.1 %reduce-scatter.2.cloned.1.call-done = bf16[3,1,256,512]{2,3,0,1:T(8,128)(2,1)} async-done(((bf16[3,4,256,512]{2,3,0,1:T(8,128)(2,1)}), bf16[3,1,256,512]{2,3,0,1:T(8,128)(2,1)}) %reduce-scatter.2.cloned.1.call-update) | async-done | bytes 786448 | tf_op jit(solution)/shard_map/reduce_scatter | solution.py:54
  107.9 1.3 bitcast_convert_fusion
  109.1 0.5 multiply_add_fusion
  109.6 0.9 slice_multiply_fusion
  110.5 1.0 copy.19
  111.5 1.2 mul.64
  112.8 1.1 fusion
  113.8 0.5 copy-done.1
  114.3 1.2 convolution_add_fusion
  115.9 12.4 %all_to_all.16 = bf16[256,4,128]{0,2,1:T(8,128)(2,1)S(1)} all-to-all(bf16[256,4,128]{0,2,1:T(8,128)(2,1)S(1)} %multiply_convert_fusion), channel_id=1, replica_groups=mesh['grp'=2,'tok'=4,'mdl'=4] {'mdl'}, dimensions={1} | all-to-all | bytes 524288 | tf_op jit(solution)/shard_map/all_to_all | solution.py:68
  128.4 0.8 copy.24
  (25 shorter events, 0.5 us)
Async XLA Ops:
  6.5 27.7 %all-gather.2.cloned.1.call-start = ((), (), s32[]{:S(2)}) async-start(), calls=%async_computation.2 | async-start | bytes 2621440 | tf_op jit(solution)/shard_map/all_gather | solution.py:47
  7.3 100.6 %reduce-scatter.2.cloned.1.call-start = ((), (), s32[]{:S(2)}) async-start(), calls=%async_computation.3 | async-start | bytes 3932160 | tf_op jit(solution)/shard_map/reduce_scatter | solution.py:54
  47.4 0.7 copy-start.4
  47.4 0.8 copy-start.3
  50.9 1.6 %slice-start = ((f32[16,32896]{1,0:T(8,128)}), f32[16,32768]{1,0:T(8,128)S(1)}, s32[]{:S(2)}) async-start(f32[16,32896]{1,0:T(8,128)} %tile.9), calls=%async_computation.4 | async-start | bytes 4194304 | tf_op jit(solution)/shard_map/slice | solution.py:11
  57.2 1.6 %slice-start.1 = ((f32[16,32896]{1,0:T(8,128)}), f32[16,32768]{1,0:T(8,128)S(1)}, s32[]{:S(2)}) async-start(f32[16,32896]{1,0:T(8,128)} %tile.21), calls=%async_computation.5 | async-start | bytes 4194304 | tf_op jit(solution)/shard_map/slice | solution.py:11
  109.6 3.2 %copy-start = (f32[2,8,128,256]{3,2,1,0:T(8,128)S(1)}, f32[2,8,128,256]{3,2,1,0:T(8,128)}, u32[]{:S(2)}) copy-start(f32[2,8,128,256]{3,2,1,0:T(8,128)} %copy.30) | copy-start | bytes 6291460
  112.7 1.6 %copy-start.1 = (f32[2,8,128,256]{3,2,1,0:T(8,128)S(1)}, f32[2,8,128,256]{3,2,1,0:T(8,128)}, u32[]{:S(2)}) copy-start(f32[2,8,128,256]{3,2,1,0:T(8,128)} %copy.31) | copy-start | bytes 6291460
  114.3 1.4 %copy-start.2 = (f32[1,256,512]{1,2,0:T(8,128)S(1)}, f32[1,256,512]{1,2,0:T(8,128)}, u32[]{:S(2)}) copy-start(f32[1,256,512]{1,2,0:T(8,128)} %get-tuple-element.6) | copy-start | bytes 1572868
  114.3 1.4 %copy-start.5 = (f32[256]{0:T(256)S(1)}, f32[256]{0:T(256)}, u32[]{:S(2)}) copy-start(f32[256]{0:T(256)} %param.9) | copy-start | bytes 3076
Sparse Core Ops, SparseCore 0:
  8.9 25.2 all-gather.1
  47.6 60.2 reduce-scatter.1

commit v2 on v1

--- a/solution.py
+++ b/solution.py
@@ -1,7 +1,13 @@
 import jax
 import jax.numpy as jnp
 from jax import lax
+from jax.experimental import pallas as pl
+from jax.experimental.pallas import tpu as pltpu
 from jax.sharding import PartitionSpec as P
+
+MESH = pl.DeviceIdType.MESH
+CHUNK = 128
+SKEW = 2
 
 
 def toeplitz_rows(padded_taps):
@@ -68,6 +74,328 @@
     return lax.all_to_all(mixed_out, "mdl", split_axis=1, concat_axis=0, tiled=True)
 
 
+def mixer_kernel(
+    tokens_ref, weight_ref, param_ref, out_ref,
+    weights, tok, inbox, outbox, summed, params, toeplitz, mixed,
+    weight_sem, tok_load_sem, tok_send_sem, tok_recv_sem,
+    param_load_sem, param_send_sem, param_recv_sem,
+    send_sem, recv_sem, mixed_send_sem, mixed_recv_sem,
+):
+    z = lax.axis_index("mdl")
+    me = lax.axis_index("tok")
+    depth = lax.axis_size("mdl")
+    rows, features = tokens_ref.shape
+    streams, channels, _ = weight_ref.shape
+    half = channels // 2
+    chunks = half // CHUNK
+    units = 4 * chunks
+    own_channels = channels // depth
+    taps = params.shape[-1]
+    group = 16
+    is_end = (z == 0) | (z == depth - 1)
+    peer = me + 1 - 2 * (me % 2)
+    across = me + 2 - 4 * (me // 2)
+    far = 3 - me
+
+    def block_rows(block):
+        return pl.ds(pl.multiple_of(block * rows, rows), rows)
+
+    def weight_copy(side, chunk):
+        window = pl.ds(side * half + chunk * CHUNK, CHUNK)
+        return pltpu.make_async_copy(
+            weight_ref.at[:, window, :], weights.at[:, window, :], weight_sem.at[side, chunk]
+        )
+
+    def token_copy(index, source, block, target):
+        return pltpu.make_async_remote_copy(
+            source, tok.at[block_rows(block), :], tok_send_sem.at[index], tok_recv_sem.at[index],
+            device_id={"tok": target}, device_id_type=MESH,
+        )
+
+    own_tokens = pltpu.make_async_copy(tokens_ref, tok.at[block_rows(me), :], tok_load_sem)
+    own_tokens.start()
+    own_params = pltpu.make_async_copy(param_ref, params.at[z % 2], param_load_sem)
+    own_params.start()
+    for chunk in range(chunks):
+        for side in range(2):
+            weight_copy(side, chunk).start()
+
+    barrier = pltpu.get_barrier_semaphore()
+    for step in range(1, depth):
+        pl.semaphore_signal(barrier, inc=1, device_id={"mdl": (z + step) % depth}, device_id_type=MESH)
+    for other in (peer, across):
+        pl.semaphore_signal(barrier, inc=1, device_id={"tok": other}, device_id_type=MESH)
+    pl.semaphore_wait(barrier, depth + 1)
+
+    to_across = token_copy(1, tokens_ref, me, across)
+    to_across.start()
+    to_peer = token_copy(0, tokens_ref, me, peer)
+    to_peer.start()
+    forward = token_copy(2, tok.at[block_rows(across), :], across, peer)
+    to_end = pltpu.make_async_remote_copy(
+        param_ref, params.at[z % 2], param_send_sem, param_recv_sem,
+        device_id={"mdl": (depth - 1) * (z // 2)}, device_id_type=MESH,
+    )
+
+    @pl.when(jnp.logical_not(is_end))
+    def _():
+        to_end.start()
+
+    own_tokens.wait()
+    own_params.wait()
+
+    def unit_copy(side, unit):
+        return pltpu.make_async_remote_copy(
+            outbox.at[side, unit], inbox.at[side, unit],
+            send_sem.at[side, unit], recv_sem.at[side, unit],
+            device_id={"mdl": (z + 2 * side - 1 + depth) % depth}, device_id_type=MESH,
+        )
+
+    def mixed_copy(chunk, step):
+        target = (z + step) % depth
+        side = z // 2
+        at_source = pl.ds(pl.multiple_of(chunk * CHUNK, CHUNK), CHUNK)
+        at_target = pl.ds(pl.multiple_of(side * half + chunk * CHUNK, CHUNK), CHUNK)
+        return pltpu.make_async_remote_copy(
+            mixed.at[target, at_source, :], out_ref.at[at_target, :],
+            mixed_send_sem.at[chunk, step - 1], mixed_recv_sem.at[side, chunk],
+            device_id={"mdl": target}, device_id_type=MESH,
+        )
+
+    def place(unit):
+        late = unit // (2 * chunks)
+        rest = unit - 2 * chunks * late
+        block = (1 - late) * (rest // chunks) + late * (2 + rest % 2)
+        chunk = (1 - late) * (rest % chunks) + late * (rest // 2)
+        return block, chunk
+
+    def block_of(order):
+        flipped_low = me % 2 + (order % 2) * (1 - 2 * (me % 2))
+        flipped_high = me // 2 + (order // 2) * (1 - 2 * (me // 2))
+        return 2 * flipped_high + flipped_low
+
+    def work(side, step):
+        position = z if side == 1 else depth - 1 - z
+        unit = step - SKEW * position
+
+        @pl.when((unit >= 0) & (unit < units))
+        def _():
+            order, chunk = place(unit)
+            block = block_of(order)
+
+            @pl.when(unit < chunks)
+            def _():
+                weight_copy(side, chunk).wait()
+
+            window = pl.ds(pl.multiple_of(side * half + chunk * CHUNK, CHUNK), CHUNK)
+            partial = lax.dot_general(
+                weights[:, window, :].reshape(streams * CHUNK, features),
+                tok[block_rows(block), :],
+                (((1,), (1,)), ((), ())),
+                preferred_element_type=jnp.float32,
+            ).reshape(streams, CHUNK, rows)
+
+            @pl.when(position == 0)
+            def _():
+                outbox[side, unit] = partial.astype(jnp.bfloat16)
+
+            @pl.when(position > 0)
+            def _():
+                unit_copy(side, unit).wait_recv()
+                total = partial + inbox[side, unit].astype(jnp.float32)
+
+                @pl.when(position < depth - 1)
+                def _():
+                    outbox[side, unit] = total.astype(jnp.bfloat16)
+
+                @pl.when(position == depth - 1)
+                def _():
+                    held = pl.ds(pl.multiple_of(chunk * CHUNK, CHUNK), CHUNK)
+                    lanes = pl.ds(pl.multiple_of(block * rows, rows), rows)
+                    summed[:, held, lanes] = total
+
+            @pl.when(position < depth - 1)
+            def _():
+                @pl.when(unit >= 2)
+                def _():
+                    unit_copy(side, unit - 2).wait_send()
+
+                unit_copy(side, unit).start()
+
+    def make_toeplitz():
+        def one(index, carry):
+            slot = index // (own_channels // group)
+            row = own_channels + index % (own_channels // group)
+            line = jnp.concatenate(
+                [params[slot, pl.ds(row, 1), :], jnp.zeros((1, taps), jnp.float32)], 1
+            )
+            wide = jnp.broadcast_to(line, (taps, 2 * taps))
+            toeplitz[index] = pltpu.roll(wide, 0, 1, stride=1, stride_axis=0).astype(jnp.bfloat16)
+            return carry
+
+        lax.fori_loop(0, half // group, one, 0)
+
+    def finish(chunk):
+        def one(index, carry):
+            channel = pl.multiple_of(chunk * CHUNK + index * group, group)
+            slot = channel // own_channels
+            row = pl.multiple_of(channel % own_channels, group)
+            held = pl.ds(channel, group)
+            scales = params[slot, pl.ds(row, group), :]
+            length = summed.shape[-1]
+            lane = lax.broadcasted_iota(jnp.int32, (group, length), 1)
+            featured = []
+            for stream in range(streams):
+                value = summed[stream, held, :]
+                feature = scales[:, 3 * stream : 3 * stream + 1] * value
+                for shift in (1, 2):
+                    moved = jnp.where(lane >= shift, pltpu.roll(value, shift, 1), 0.0)
+                    at = 3 * stream + shift
+                    feature = feature + scales[:, at : at + 1] * moved
+                featured.append(feature)
+            product = featured[1] * featured[2]
+            blocks = length // taps
+            stacked = jnp.concatenate(
+                [product[:, n * taps : (n + 1) * taps] for n in range(blocks)], 0
+            ).astype(jnp.bfloat16)
+            spread = jnp.dot(
+                stacked, toeplitz[channel // group], preferred_element_type=jnp.float32
+            )
+            for n in range(blocks):
+                near = spread[n * group : (n + 1) * group, :taps]
+                if n > 0:
+                    near = near + spread[(n - 1) * group : n * group, taps:]
+                cut = slice(n * taps, (n + 1) * taps)
+                gated = featured[0][:, cut] * (near + scales[:, 9:10] * product[:, cut])
+                mixed[n, held, :] = gated.astype(jnp.bfloat16)
+            return carry
+
+        lax.fori_loop(0, CHUNK // group, one, 0)
+        at_source = pl.ds(pl.multiple_of(chunk * CHUNK, CHUNK), CHUNK)
+        at_target = pl.ds(pl.multiple_of((z // 2) * half + chunk * CHUNK, CHUNK), CHUNK)
+        for step in range(1, depth):
+            mixed_copy(chunk, step).start()
+        out_ref[at_target, :] = mixed[z, at_source, :]
+
+    def timestep(step, carry):
+        @pl.when(step == chunks)
+        def _():
+            to_peer.wait_recv()
+
+        @pl.when(step == 2 * chunks - 1)
+        def _():
+            to_across.wait_recv()
+            forward.start()
+
+        @pl.when(step == 2 * chunks + 1)
+        def _():
+            forward.wait_recv()
+
+        work(0, step)
+        work(1, step)
+
+        @pl.when(is_end & (step == 3))
+        def _():
+            pltpu.make_async_remote_copy(
+                param_ref, params.at[(z + 1) % 2], param_send_sem, param_recv_sem,
+                device_id={"mdl": (z + 1) % depth}, device_id_type=MESH,
+            ).wait_recv()
+            make_toeplitz()
+
+        unit = step - SKEW * (depth - 1)
+
+        @pl.when(is_end & (unit >= 2 * chunks) & (unit % 2 == 1))
+        def _():
+            finish((unit - 2 * chunks) // 2)
+
+        return carry
+
+    lax.fori_loop(0, units + SKEW * (depth - 1), timestep, 0)
+
+    to_across.wait_send()
+    to_peer.wait_send()
+    forward.wait_send()
+
+    @pl.when(jnp.logical_not(is_end))
+    def _():
+        to_end.wait_send()
+
+    for side in range(2):
+        position = z if side == 1 else depth - 1 - z
+
+        @pl.when(position < depth - 1)
+        def _():
+            unit_copy(side, units - 2).wait_send()
+            unit_copy(side, units - 1).wait_send()
+
+        @pl.when(position < depth - 1)
+        def _():
+            for chunk in range(chunks):
+                window = pl.ds(side * half + chunk * CHUNK, CHUNK)
+                pltpu.make_async_remote_copy(
+                    mixed.at[0, pl.ds(chunk * CHUNK, CHUNK), :], out_ref.at[window, :],
+                    mixed_send_sem.at[chunk, 0], mixed_recv_sem.at[side, chunk],
+                    device_id={"mdl": (z + 1) % depth}, device_id_type=MESH,
+                ).wait_recv()
+
+    @pl.when(is_end)
+    def _():
+        for chunk in range(chunks):
+            for step in range(1, depth):
+                mixed_copy(chunk, step).wait_send()
+
+
+def local_fused(tokens, in_weight, short_weight, long_filter, skip_bias):
+    depth = lax.axis_size("mdl")
+    rows, features = tokens.shape
+    channels, streams, _ = in_weight.shape
+    groups, taps = long_filter.shape
+    own_channels = channels // depth
+    half = channels // 2
+    chunks = half // CHUNK
+    units = 4 * chunks
+    length = rows * lax.axis_size("tok")
+    scales = jnp.concatenate([short_weight.reshape(own_channels, streams * 3), skip_bias[:, None]], 1)
+    scales = jnp.pad(scales, ((0, 0), (0, taps - scales.shape[1])))
+    params = jnp.concatenate([scales, long_filter], 0)
+    dma = pltpu.SemaphoreType.DMA
+    return pl.pallas_call(
+        mixer_kernel,
+        out_shape=jax.ShapeDtypeStruct((channels, length // depth), jnp.bfloat16),
+        in_specs=[pl.BlockSpec(memory_space=pl.ANY)] * 3,
+        out_specs=pl.BlockSpec(memory_space=pltpu.VMEM),
+        scratch_shapes=[
+            pltpu.VMEM((streams, channels, features), jnp.bfloat16),
+            pltpu.VMEM((length, features), jnp.bfloat16),
+            pltpu.VMEM((2, units, streams, CHUNK, rows), jnp.bfloat16),
+            pltpu.VMEM((2, units, streams, CHUNK, rows), jnp.bfloat16),
+            pltpu.VMEM((streams, half, length), jnp.float32),
+            pltpu.VMEM((2, own_channels + groups, taps), jnp.float32),
+            pltpu.VMEM((half // 16, taps, 2 * taps), jnp.bfloat16),
+            pltpu.VMEM((depth, half, length // depth), jnp.bfloat16),
+            dma((2, chunks)),
+            dma,
+            dma((3,)),
+            dma((3,)),
+            dma,
+            dma,
+            dma,
+            dma((2, units)),
+            dma((2, units)),
+            dma((chunks, depth - 1)),
+            dma((2, chunks)),
+        ],
+        compiler_params=pltpu.CompilerParams(
+            collective_id=0, has_side_effects=True, vmem_limit_bytes=52 * 1024 * 1024
+        ),
+        cost_estimate=pl.CostEstimate(
+            flops=2 * length * streams * channels * features,
+            bytes_accessed=2 * streams * channels * features,
+            transcendentals=0,
+        ),
+    )(tokens, in_weight.transpose(1, 0, 2), params)
+
+
 def solution(mesh):
     in_specs = (
         P(("grp", "tok"), "mdl"),
@@ -77,4 +405,5 @@
         P(("tok", "mdl")),
     )
     out_specs = P("tok", ("grp", "mdl"))
-    return jax.shard_map(local, mesh=mesh, in_specs=in_specs, out_specs=out_specs, check_vma=False)
+    body = local_fused if mesh.shape["mdl"] == 4 and mesh.shape["tok"] == 4 else local
+    return jax.shard_map(body, mesh=mesh, in_specs=in_specs, out_specs=out_specs, check_vma=False)

time: 136 us -> 64.9 us (0.48)
  waiting for transfers between devices: 74.8 us -> 0 us
  Pallas kernels: 0 us -> 60.6 us
  local copies, waits for them, and re-layouts: 19.8 us -> 2.58 us
  between operations: 13.6 us -> 0.02 us
  matrix products: 12.6 us -> 0 us
  blocking collectives: 12.4 us -> 0 us
  other arithmetic: 2.76 us -> 1.39 us
    pallas_call x0 -> x1, Pallas kernels: none -> 60.6 us  [local_fused(): pl.pallas_call(mixer_kernel, out_shape=jax.ShapeDtypeStruct((channels, le...]
    reduce_scatter x1 -> x0, waiting for transfers between devices: 47.1 us -> none  [local(): streams = lax.psum_scatter(partial, 'mdl', scatter_dimension=1, tiled=True)]
    all_gather x1 -> x0, waiting for transfers between devices: 26.9 us -> none  [local(): gathered = lax.all_gather(tokens, 'tok', axis=0, tiled=True)]
    dot_general x3 -> x0, matrix products: 12.6 us -> none  [the longest x1 10.4 us: local(): lax.dot_general(weight_rows, gathered, (((1,), (1,)), ((), ())), preferre...]
    all_to_all x1 -> x0, blocking collectives: 12.4 us -> none  [local(): lax.all_to_all(mixed_out, 'mdl', split_axis=1, concat_axis=0, tiled=True)]
    another operation x4 -> x0, local copies, waits for them, and re-layouts: 5.41 us -> none  [toeplitz_rows(): tiled = jnp.tile(padded_taps, (1, tap_count))]
    unnamed x16 -> x3, local copies, waits for them, and re-layouts: 5.14 us -> 1.74 us
    slice x5 -> x0, local copies, waits for them, and re-layouts: 3.19 us -> none  [the longest x4 3.18 us: toeplitz_rows(): trimmed = tiled[:, :tap_count * (padded_len - 1)]]
  transfers between devices with their start and end apart: 2 -> 0, of which waited for: 2 -> 0; matrix products, arithmetic and copies ran while one was open for 7% -> 0% of each run, Pallas kernels for 0% -> 0%
where the time goes in v2:
time: 64.9 us; the launch traced here: 64.6 us
  Pallas kernels  60.6 us (93%)
  local copies, waits for them, and re-layouts  2.58 us (4%)
  other arithmetic  1.39 us (2%)
    pallas_call x1, Pallas kernels, local_fused(): pl.pallas_call(mixer_kernel, out_shape=jax.ShapeDtypeStruct((channels, le...  60.6 us
    unnamed x3, local copies, waits for them, and re-layouts  1.74 us

profile of v2, /device:TPU:0, one launch (start us, length us, event | category | flops | bytes accessed | tf_op | source)
XLA Modules:
  0.0 64.6 jit_solution(12679123191271642640)
XLA Ops:
  0.0 0.7 %reshape.3 = f32[256,9]{0,1:T(8,128)S(1)} reshape(f32[256,3,3]{0,2,1:T(4,128)} %param.7) | data formatting | bytes 18432 | tf_op jit(solution)/shard_map/reshape | solution.py:358
  0.7 0.7 %pad_maximum_fusion = f32[256,10]{0,1:T(8,128)S(1)} fusion(f32[256,1]{0,1:T(1,128)} %bitcast.4, f32[256,9]{0,1:T(8,128)S(1)} %reshape.3), kind=kLoop, calls=%fused_computation.2 | loop fusion | flops 2560 | bytes 20480 | tf_op jit(solution)/shard_map/concatenate | solution.py:358
  1.4 0.1 copy.9
  1.5 0.7 %select_maximum_fusion.param_ref = f32[272,128]{1,0:T(8,128)S(1)} fusion(f32[256,10]{1,0:T(8,128)S(1)} %copy.9, f32[16,128]{1,0:T(8,128)} %param.8), kind=kLoop, calls=%fused_computation | loop fusion | flops 104448 | bytes 157696 | tf_op jit(solution)/shard_map/concatenate | solution.py:360
  2.2 0.0 copy-start
  2.2 1.0 %copy-done = bf16[128,2048]{1,0:T(8,128)(2,1)S(1)} copy-done((bf16[128,2048]{1,0:T(8,128)(2,1)S(1)}, bf16[128,2048]{1,0:T(8,128)(2,1)}, u32[]{:S(2)}) %copy-start) | copy-done | bytes 524312
  3.3 60.6 %shard_map.55 = bf16[1024,128]{1,0:T(8,128)(2,1)S(1)} custom-call(bf16[128,2048]{1,0:T(8,128)(2,1)S(1)} %copy-done, bf16[3,1024,2048]{2,1,0:T(8,128)(2,1)} %bitcast.5, f32[272,128]{1,0:T(8,128)S(1)} %select_maximum_fusion.param_ref), custom_call_target="tpu_custom_call" | custom-call | flops 6442450944 | bytes 12582912 | tf_op jit(solution)/shard_map/pallas_call | solution.py:362
  63.9 0.7 %copy.11 = bf16[1024,128]{1,0:T(8,128)(2,1)} copy(bf16[1024,128]{1,0:T(8,128)(2,1)S(1)} %shard_map.55) | data formatting | bytes 524288
Async XLA Ops:
  2.2 1.0 %copy-start = (bf16[128,2048]{1,0:T(8,128)(2,1)S(1)}, bf16[128,2048]{1,0:T(8,128)(2,1)}, u32[]{:S(2)}) copy-start(bf16[128,2048]{1,0:T(8,128)(2,1)} %tokens_ref.1) | copy-start | bytes 1572868

commit v3 on v2

--- a/solution.py
+++ b/solution.py
@@ -8,6 +8,7 @@
 MESH = pl.DeviceIdType.MESH
 CHUNK = 128
 SKEW = 2
+AHEAD = 8
 
 
 def toeplitz_rows(padded_taps):
@@ -216,9 +217,9 @@
 
             @pl.when(position < depth - 1)
             def _():
-                @pl.when(unit >= 2)
+                @pl.when(unit >= AHEAD)
                 def _():
-                    unit_copy(side, unit - 2).wait_send()
+                    unit_copy(side, unit - AHEAD).wait_send()
 
                 unit_copy(side, unit).start()
 
@@ -325,8 +326,8 @@
 
         @pl.when(position < depth - 1)
         def _():
-            unit_copy(side, units - 2).wait_send()
-            unit_copy(side, units - 1).wait_send()
+            for last in range(AHEAD):
+                unit_copy(side, units - AHEAD + last).wait_send()
 
         @pl.when(position < depth - 1)
         def _():

time: 64.9 us -> 62.7 us (0.966)
  Pallas kernels: 60.6 us -> 58.4 us
    pallas_call x1, Pallas kernels: 60.6 us -> 58.4 us  [local_fused(): pl.pallas_call(mixer_kernel, out_shape=jax.ShapeDtypeStruct((channels, le...]
where the time goes in v3:
time: 62.7 us; the launch traced here: 62.4 us
  Pallas kernels  58.4 us (93%)
  local copies, waits for them, and re-layouts  2.58 us (4%)
  other arithmetic  1.39 us (2%)
    pallas_call x1, Pallas kernels, local_fused(): pl.pallas_call(mixer_kernel, out_shape=jax.ShapeDtypeStruct((channels, le...  58.4 us
    unnamed x3, local copies, waits for them, and re-layouts  1.74 us

profile of v3, /device:TPU:0, one launch (start us, length us, event | category | flops | bytes accessed | tf_op | source)
XLA Modules:
  0.0 62.4 jit_solution(5461464367481687525)
XLA Ops:
  0.0 0.7 %reshape.3 = f32[256,9]{0,1:T(8,128)S(1)} reshape(f32[256,3,3]{0,2,1:T(4,128)} %param.7) | data formatting | bytes 18432 | tf_op jit(solution)/shard_map/reshape | solution.py:359
  0.7 0.7 %pad_maximum_fusion = f32[256,10]{0,1:T(8,128)S(1)} fusion(f32[256,1]{0,1:T(1,128)} %bitcast.4, f32[256,9]{0,1:T(8,128)S(1)} %reshape.3), kind=kLoop, calls=%fused_computation.2 | loop fusion | flops 2560 | bytes 20480 | tf_op jit(solution)/shard_map/concatenate | solution.py:359
  1.4 0.1 copy.9
  1.5 0.7 %select_maximum_fusion.param_ref = f32[272,128]{1,0:T(8,128)S(1)} fusion(f32[256,10]{1,0:T(8,128)S(1)} %copy.9, f32[16,128]{1,0:T(8,128)} %param.8), kind=kLoop, calls=%fused_computation | loop fusion | flops 104448 | bytes 157696 | tf_op jit(solution)/shard_map/concatenate | solution.py:361
  2.2 0.0 copy-start
  2.2 1.0 %copy-done = bf16[128,2048]{1,0:T(8,128)(2,1)S(1)} copy-done((bf16[128,2048]{1,0:T(8,128)(2,1)S(1)}, bf16[128,2048]{1,0:T(8,128)(2,1)}, u32[]{:S(2)}) %copy-start) | copy-done | bytes 524312
  3.3 58.4 %shard_map.55 = bf16[1024,128]{1,0:T(8,128)(2,1)S(1)} custom-call(bf16[128,2048]{1,0:T(8,128)(2,1)S(1)} %copy-done, bf16[3,1024,2048]{2,1,0:T(8,128)(2,1)} %bitcast.5, f32[272,128]{1,0:T(8,128)S(1)} %select_maximum_fusion.param_ref), custom_call_target="tpu_custom_call" | custom-call | flops 6442450944 | bytes 12582912 | tf_op jit(solution)/shard_map/pallas_call | solution.py:363
  61.7 0.7 %copy.11 = bf16[1024,128]{1,0:T(8,128)(2,1)} copy(bf16[1024,128]{1,0:T(8,128)(2,1)S(1)} %shard_map.55) | data formatting | bytes 524288
Async XLA Ops:
  2.2 1.0 %copy-start = (bf16[128,2048]{1,0:T(8,128)(2,1)S(1)}, bf16[128,2048]{1,0:T(8,128)(2,1)}, u32[]{:S(2)}) copy-start(bf16[128,2048]{1,0:T(8,128)(2,1)} %tokens_ref.1) | copy-start | bytes 1572868
